TPU v7x, 32 devices: a whole 2x2x4 slice. The times are simulated.
32 devices in a mesh: parts: 2 (over x), rows: 16 (over z, y, core).
Axes of the slice: x: 2, y: 2, z: 4, core: 2. Of those that a mesh axis runs over, the one named last changes fastest.
Arguments:
- lap_tiles: float32 [512, 7, 128, 128], P(('parts', 'rows')), parts along dimension 0, may hold values from -91.799777 to 91.799777, as said below
- tile_columns: int32 [512, 7], P(('parts', 'rows')), parts along dimension 0, may hold values from 0 to 255, as said below
- start_block: float32 [65536, 64], P(('parts', 'rows')), parts along dimension 0, may hold values from -6 to 6
- patch_of: int32 [65536, 1], P(('parts', 'rows')), parts along dimension 0, may hold values from 0 to 63; in each aligned block of 2048 rows (0 to 2047, 2048 to 4095, ...) at most 64 rows name the same one
- mix_weight: bfloat16 [128, 256], replicated, may hold values from -0.5 to 0.5
- class_weight: bfloat16 [256, 16], replicated, may hold values from -0.375 to 0.375
Outputs:
- embedding: bfloat16 [65536, 64], P(('parts', 'rows')), parts along dimension 0
- ritz: float32 [128, 64], P('parts'), parts along dimension 0
- labels: bfloat16 [65536, 16], P(('parts', 'rows')), parts along dimension 0
There are 2 independent parts, one for each index of `parts`. A program takes and returns all parts, laid end to end along the dimension named above; an argument that names none is the same for every part. Nothing has to cross between parts.
Inputs may be any that keep to these rules, and one draw needn't show every extreme that they name: L is symmetric: where tile_columns[b, t] = c, block c has a tile with column block b, and that tile is the transpose of lap_tiles[b, t]. Each vertex's row of L, over all tiles of its row block, sums to zero. `tile_columns`: tile 0 of row block b has column block b; the tiles of one row block name distinct column blocks, each among the device's own row blocks or within 2 row blocks beyond them on either side, counted cyclically over the 256 blocks. `patch_of`: among the 2048 vertices of one device no patch occurs more than 64 times; every patch has at least one vertex.
All inputs are finite; a program needn't handle non-finite values.
Results may differ from a plain program's by a relative error of at most 0.0058.
Values may be sent and summed in bfloat16 or wider, within the bound.
A program may use at most 64 MiB of HBM per device.

v0:
```python
import math

import jax
import jax.numpy as jnp
from jax import lax
from jax.sharding import PartitionSpec as P

HALO_BLOCKS = 2
PATCH_DEV = 4


highest_precision = lax.Precision.HIGHEST


def extended(x, sides, width):
    for axis, dim in sides:
        count, length = (lax.axis_size(axis), x.shape[dim])
        up = [(i, (i + 1) % count) for i in range(count)]
        down = [(j, i) for i, j in up]
        last = lax.slice_in_dim(x, length - width, length, axis=dim)
        initial = lax.slice_in_dim(x, 0, width, axis=dim)
        before = lax.ppermute(last, axis, up)
        after = lax.ppermute(initial, axis, down)
        x = jnp.concatenate([before, x, after], axis=dim)
    return x


def apply_local(vectors, lap_tiles, tile_columns):
    blocks_here = lap_tiles.shape[0]
    tile_side = lap_tiles.shape[2]
    columns = vectors.shape[1]
    total_blocks = blocks_here * lax.axis_size("rows")
    padded = extended(vectors, (("rows", 0),), HALO_BLOCKS * tile_side)
    padded_blocks = padded.reshape(-1, tile_side, columns)
    base_block = lax.axis_index("rows") * blocks_here - HALO_BLOCKS
    picked = padded_blocks[(tile_columns - base_block) % total_blocks]
    product = jnp.einsum("btij,btjk->bik", lap_tiles, picked, precision=highest_precision)
    return (4.0 * vectors.reshape(blocks_here, tile_side, columns) - product).reshape(vectors.shape)


def inner_matrix(left, right):
    return jnp.dot(left.T, right, precision=highest_precision, preferred_element_type=jnp.float32)


def gram_factor(vectors):
    moment = lax.psum(inner_matrix(vectors, vectors), "rows")
    return jnp.linalg.cholesky(moment)


def apply_inverse(vectors, factor):
    return jax.scipy.linalg.solve_triangular(factor, vectors.T, lower=True).T


def on_device(lap_tiles, tile_columns, start_block, patch_of, mix_weight, class_weight):
    devices = lax.axis_size("rows")
    rows_here = start_block.shape[0]
    width = start_block.shape[1]
    first_image = apply_local(start_block, lap_tiles, tile_columns)
    first_basis = apply_inverse(first_image, gram_factor(first_image))
    second_image = apply_local(first_basis, lap_tiles, tile_columns)
    basis = apply_inverse(second_image, gram_factor(second_image))
    image = apply_local(basis, lap_tiles, tile_columns)
    ritz = lax.psum(inner_matrix(basis, image), "rows")
    scale = math.sqrt(rows_here * devices)
    scaled = scale * jnp.dot(
        basis, ritz, precision=highest_precision, preferred_element_type=jnp.float32
    )
    embedding = scaled.astype(jnp.bfloat16)
    patch_ids = patch_of[:, 0]
    patches = PATCH_DEV * devices
    capacity = max(2, 2 * rows_here // patches)
    member_int = (patch_ids[:, None] == jnp.arange(patches, dtype=jnp.int32)[None, :]).astype(
        jnp.int32
    )
    running = jnp.cumsum(member_int, axis=0)
    rank = jnp.sum(running * member_int, axis=1) - 1
    counts = jnp.sum(member_int, axis=0).reshape(devices, PATCH_DEV)
    slot = patch_ids * capacity + rank
    outgoing = jnp.zeros((patches * capacity, width), jnp.bfloat16).at[slot].set(embedding)
    outgoing = outgoing.reshape(devices, PATCH_DEV * capacity, width)
    arrived, arrived_counts = (
        lax.all_to_all(outgoing, "rows", split_axis=0, concat_axis=0, tiled=True),
        lax.all_to_all(counts, "rows", split_axis=0, concat_axis=0, tiled=True),
    )
    grouped = arrived.reshape(devices, PATCH_DEV, capacity, width)
    valid = (
        jnp.arange(capacity, dtype=jnp.int32)[None, None, :] < arrived_counts[:, :, None]
    ).astype(jnp.bfloat16)
    sums = jnp.einsum("spc,spck->pk", valid, grouped, preferred_element_type=jnp.float32)
    totals = jnp.sum(arrived_counts, axis=0).astype(jnp.float32)
    patch_mean = (sums / totals[:, None]).astype(jnp.bfloat16)
    mean_project = jnp.dot(patch_mean, mix_weight[width:], preferred_element_type=jnp.float32)
    arrived_project = jnp.dot(
        arrived.reshape(-1, width), mix_weight[:width], preferred_element_type=jnp.float32
    )
    before = (
        arrived_project.reshape(devices, PATCH_DEV, capacity, -1) + mean_project[None, :, None, :]
    )
    hidden = jax.nn.gelu(before, approximate=False).astype(jnp.bfloat16)
    scores = jnp.dot(
        hidden.reshape(-1, hidden.shape[-1]), class_weight, preferred_element_type=jnp.float32
    )
    scores = scores.astype(jnp.bfloat16).reshape(devices, PATCH_DEV * capacity, -1)
    returned = lax.all_to_all(scores, "rows", split_axis=0, concat_axis=0, tiled=True)
    labels = returned.reshape(-1, returned.shape[-1])[slot]
    return (embedding, ritz, labels)


def solution(mesh):
    in_specs = (
        P(("parts", "rows"), None, None, None),
        P(("parts", "rows"), None),
        P(("parts", "rows"), None),
        P(("parts", "rows"), None),
        P(),
        P(),
    )
    out_specs = (P(("parts", "rows"), None), P("parts", None), P(("parts", "rows"), None))
    return jax.shard_map(
        on_device, mesh=mesh, in_specs=in_specs, out_specs=out_specs, check_vma=False
    )
```

profile of v0, /device:TPU:0, one launch (start us, length us, event | category | flops | bytes accessed | tf_op | source)
XLA Modules:
  0.0 357.5 jit_solution(16470783498688638745)
XLA Ops:
  0.7 0.9 fusion.46
  2.1 5.1 %collective-permute-start.1 = (f32[256,64]{0,1:T(8,128)S(1)}, f32[256,64]{0,1:T(8,128)S(1)}, u32[]{:S(2)}, u32[]{:S(2)}) collective-permute-start(f32[256,64]{0,1:T(8,128)S(1)} %get-tuple-element.21), channel_id=1, source_target_pairs={{1,0},{2,1},{3,2},{4,3},{5,4},{6,5},{7,6},{8,7},{9,8},{10,9},{11,1... | collective-permute-start | bytes 196616 | tf_op jit(solution)/shard_map/ppermute | solution.py:23
  7.2 0.7 fusion.27
  7.9 18.1 %reduce-window.6 = s32[64,16,128]{2,1,0:T(8,128)S(1)} reduce-window(s32[64,16,128]{2,1,0:T(8,128)S(1)} %fusion.27, s32[]{:T(128)} %constant.104.clone.1), window={size=1x1x128 pad=0_0x0_0x127_0}, to_apply=%region_5.8 | reduce-window | flops 16646144 | bytes 1048580 | tf_op jit(solution)/shard_map/reduce-window
  27.4 0.7 all_to_all.13
  28.1 3.6 %all-to-all-start.1 = ((s32[16,1,4]{2,1,0:T(1,128)}), s32[16,1,4]{2,1,0:T(1,128)S(1)}, u32[]{:S(2)}, u32[]{:S(2)}) async-start(s32[16,1,4]{2,1,0:T(1,128)} %bitcast.35), calls=%async_computation.1 | async-start | bytes 16384 | tf_op jit(solution)/shard_map/all_to_all | solution.py:83
  32.1 2.6 gather_fusion
  34.7 11.2 %fusion.11 = f32[16,128,64]{1,2,0:T(8,128)S(1)} fusion(f32[16,7,128,64]{2,3,1,0:T(8,128)} %bitcast.166, f32[16,7,128,128]{3,2,1,0:T(8,128)} %param.9, f32[2048,64]{0,1:T(8,128)S(1)} %copy-done.1), kind=kOutput, calls=%fused_computation.31 | convolution fusion | flops 1409548288 | bytes 12058624 | tf_op jit(solution)/shard_map/btij,btjk->bik/dot_general | solution.py:37
  46.5 61.9 %psum.21 = f32[64,64]{0,1:T(8,128)S(1)} all-reduce(f32[64,64]{0,1:T(8,128)S(1)} %convolution_bitcast_fusion.5), channel_id=1, replica_groups=mesh['parts'=2,'rows'=16] {'rows'}, use_global_device_ids=true, to_apply=%region_0.1 | all-reduce | flops 4096 | bytes 32768 | tf_op jit(solution)/shard_map/psum | solution.py:46
  108.4 5.8 %cholesky.44 = f32[64,64]{1,0:T(8,128)S(1)} custom-call(f32[64,64]{1,0:T(8,128)S(1)} %fusion.35), custom_call_target="Cholesky" | custom-call | tf_op jit(solution)/shard_map/jit(cholesky)/cholesky | solution.py:47
  115.6 4.9 %custom-call.6 = f32[1,64,64]{1,2,0:T(8,128)S(1)} custom-call(f32[1,64,64]{2,1,0:T(8,128)S(1)} %fusion.29), custom_call_target="InvertDiagBlocksLowerTriangular" | custom-call | tf_op jit(solution)/shard_map/jit(_solve_triangular)/triangular_solve | solution.py:51
  121.3 4.4 %collective-permute-start.3 = (f32[256,64]{0,1:T(8,128)S(1)}, f32[256,64]{0,1:T(8,128)S(1)}, u32[]{:S(2)}, u32[]{:S(2)}) collective-permute-start(f32[256,64]{0,1:T(8,128)S(1)} %get-tuple-element.19), channel_id=1, source_target_pairs={{1,0},{2,1},{3,2},{4,3},{5,4},{6,5},{7,6},{8,7},{9,8},{10,9},{11,1... | collective-permute-start | bytes 196616 | tf_op jit(solution)/shard_map/ppermute | solution.py:23
  125.7 1.9 collective-permute-done.2
  127.7 2.6 gather_fusion.1
  130.3 11.2 %fusion.12 = f32[16,128,64]{1,2,0:T(8,128)S(1)} fusion(f32[16,7,128,64]{2,3,1,0:T(8,128)} %bitcast.164, f32[16,7,128,128]{3,2,1,0:T(8,128)} %param.9, f32[2048,64]{0,1:T(8,128)S(1)} %convolution_bitcast_fusion), kind=kOutput, calls=%fused_computation.32 | convolution fusion | flops 1409548288 | bytes 12058624 | tf_op jit(solution)/shard_map/btij,btjk->bik/dot_general | solution.py:37
  142.1 62.0 %psum.22 = f32[64,64]{0,1:T(8,128)S(1)} all-reduce(f32[64,64]{0,1:T(8,128)S(1)} %convolution_bitcast_fusion.4), channel_id=1, replica_groups=mesh['parts'=2,'rows'=16] {'rows'}, use_global_device_ids=true, to_apply=%region_3.6 | all-reduce | flops 4096 | bytes 32768 | tf_op jit(solution)/shard_map/psum | solution.py:46
  204.2 5.8 %cholesky.55 = f32[64,64]{1,0:T(8,128)S(1)} custom-call(f32[64,64]{1,0:T(8,128)S(1)} %fusion.33), custom_call_target="Cholesky" | custom-call | tf_op jit(solution)/shard_map/jit(cholesky)/cholesky | solution.py:47
  211.3 4.9 %custom-call.7 = f32[1,64,64]{1,2,0:T(8,128)S(1)} custom-call(f32[1,64,64]{2,1,0:T(8,128)S(1)} %fusion.30), custom_call_target="InvertDiagBlocksLowerTriangular" | custom-call | tf_op jit(solution)/shard_map/jit(_solve_triangular)/triangular_solve | solution.py:51
  217.0 4.4 %collective-permute-start.5 = (f32[256,64]{0,1:T(8,128)S(1)}, f32[256,64]{0,1:T(8,128)S(1)}, u32[]{:S(2)}, u32[]{:S(2)}) collective-permute-start(f32[256,64]{0,1:T(8,128)S(1)} %get-tuple-element.17), channel_id=1, source_target_pairs={{1,0},{2,1},{3,2},{4,3},{5,4},{6,5},{7,6},{8,7},{9,8},{10,9},{11,1... | collective-permute-start | bytes 196616 | tf_op jit(solution)/shard_map/ppermute | solution.py:23
  221.4 1.9 collective-permute-done.4
  223.4 2.6 gather_fusion.2
  226.0 11.2 %fusion.14 = f32[16,8,8,128]{3,2,1,0:T(8,128)S(1)} fusion(f32[16,7,128,64]{2,3,1,0:T(8,128)} %bitcast.165, f32[16,7,128,128]{3,2,1,0:T(8,128)} %param.9, f32[64,2048]{1,0:T(8,128)S(1)} %fusion.22), kind=kOutput, calls=%fused_computation.34 | convolution fusion | flops 1409548288 | bytes 12058624 | tf_op jit(solution)/shard_map/btij,btjk->bik/dot_general | solution.py:37
  237.8 62.1 %psum.23 = f32[64,64]{1,0:T(8,128)S(1)} all-reduce(f32[64,64]{1,0:T(8,128)S(1)} %fusion.19), channel_id=1, replica_groups=mesh['parts'=2,'rows'=16] {'rows'}, use_global_device_ids=true, to_apply=%region_4.7 | all-reduce | flops 4096 | bytes 32768 | tf_op jit(solution)/shard_map/psum | solution.py:63
  300.8 6.1 %scatter_custom_fusion = bf16[4096,64]{1,0:T(8,128)(2,1)S(1)} fusion(s32[2048]{0:T(1024)S(1)} %bitcast.181, bf16[2048,64]{1,0:T(8,128)(2,1)S(1)} %copy.60, bf16[]{:T(256)} %constant.109.clone.1), kind=kCustom, calls=%fused_computation.59 | custom fusion | bytes 524290 | tf_op jit(solution)/shard_map/scatter | solution.py:79
  306.9 1.2 copy.61
  308.1 3.6 all-to-all-start
  311.8 14.3 %all-to-all-done = bf16[16,256,64]{1,2,0:T(8,128)(2,1)S(1)} async-done(((bf16[16,256,64]{1,2,0:T(8,128)(2,1)}), bf16[16,256,64]{1,2,0:T(8,128)(2,1)S(1)}, u32[]{:S(2)}, u32[]{:S(2)}) %all-to-all-start) | async-done | bytes 524320 | tf_op jit(solution)/shard_map/all_to_all | solution.py:82
  327.1 9.6 %fusion.2 = bf16[16,4,64,256]{3,2,1,0:T(8,128)(2,1)S(1)} fusion(bf16[16,4,64,64]{3,2,1,0:T(8,128)(2,1)S(1)} %bitcast.174, f32[4,256]{1,0:T(4,128)S(1)} %fusion.38, bf16[128,256]{1,0:T(8,128)(2,1)S(1)} %copy-done.6), kind=kOutput, calls=%fused_computation.9 | convolution fusion | flops 203423744 | bytes 3182592 | tf_op jit(solution)/shard_map/dot_general | solution.py:93
  338.1 4.0 %all-to-all-start.2 = ((bf16[16,256,16]{1,2,0:T(8,128)(2,1)}), bf16[16,256,16]{1,2,0:T(8,128)(2,1)S(1)}, u32[]{:S(2)}, u32[]{:S(2)}) async-start(bf16[16,256,16]{1,2,0:T(8,128)(2,1)} %bitcast.162), calls=%async_computation.2 | async-start | bytes 262144 | tf_op jit(solution)/shard_map/all_to_all | solution.py:104
  342.1 7.9 %all-to-all-done.2 = bf16[16,256,16]{1,2,0:T(8,128)(2,1)S(1)} async-done(((bf16[16,256,16]{1,2,0:T(8,128)(2,1)}), bf16[16,256,16]{1,2,0:T(8,128)(2,1)S(1)}, u32[]{:S(2)}, u32[]{:S(2)}) %all-to-all-start.2) | async-done | bytes 131104 | tf_op jit(solution)/shard_map/all_to_all | solution.py:104
  350.5 6.2 %gather_fusion.3 = bf16[2048,16]{1,0:T(8,128)(2,1)S(1)} fusion(bf16[4096,16]{1,0:T(8,128)(2,1)S(1)} %bitcast.167, s32[2048]{0:T(1024)S(1)} %broadcast_clamp_fusion), kind=kCustom, calls=%fused_computation.3 | custom fusion | bytes 139264 | tf_op jit(solution)/shard_map/gather | solution.py:105
  356.7 0.8 copy.68
  (65 shorter events, 12.0 us)
Async XLA Ops:
  0.6 336.1 %copy-start = (bf16[256,16]{0,1:T(8,128)(2,1)S(1)}, bf16[256,16]{0,1:T(8,128)(2,1)}, u32[]{:S(2)}) copy-start(bf16[256,16]{0,1:T(8,128)(2,1)} %param.14) | copy-start | bytes 24580
  0.6 31.3 %copy-start.1 = (f32[2048,64]{0,1:T(8,128)S(1)}, f32[2048,64]{0,1:T(8,128)}, u32[]{:S(2)}) copy-start(f32[2048,64]{0,1:T(8,128)} %param.11) | copy-start | bytes 1572868
  0.7 26.4 %copy-start.4 = (s32[2048,1]{0,1:T(1,128)S(1)}, s32[2048,1]{0,1:T(1,128)}, u32[]{:S(2)}) copy-start(s32[2048,1]{0,1:T(1,128)} %param.12) | copy-start | bytes 24580
  0.7 31.1 %copy-start.5 = (s32[16,7]{0,1:T(8,128)S(1)}, s32[16,7]{0,1:T(8,128)}, u32[]{:S(2)}) copy-start(s32[16,7]{0,1:T(8,128)} %param.10) | copy-start | bytes 1348
  1.6 30.4 %collective-permute-start = (f32[256,64]{0,1:T(8,128)S(1)}, f32[256,64]{0,1:T(8,128)S(1)}, u32[]{:S(2)}, u32[]{:S(2)}) collective-permute-start(f32[256,64]{0,1:T(8,128)S(1)} %get-tuple-element.20), channel_id=1, source_target_pairs={{0,1},{1,2},{2,3},{3,4},{4,5},{5,6},{6,7},{7,8},{8,9},{9,10},{10,1... | collective-permute-start | bytes 196616 | tf_op jit(solution)/shard_map/ppermute | solution.py:22
  2.1 29.9 %collective-permute-start.1 = (f32[256,64]{0,1:T(8,128)S(1)}, f32[256,64]{0,1:T(8,128)S(1)}, u32[]{:S(2)}, u32[]{:S(2)}) collective-permute-start(f32[256,64]{0,1:T(8,128)S(1)} %get-tuple-element.21), channel_id=1, source_target_pairs={{1,0},{2,1},{3,2},{4,3},{5,4},{6,5},{7,6},{8,7},{9,8},{10,9},{11,1... | collective-permute-start | bytes 196616 | tf_op jit(solution)/shard_map/ppermute | solution.py:23
  28.1 279.9 %all-to-all-start.1 = ((s32[16,1,4]{2,1,0:T(1,128)}), s32[16,1,4]{2,1,0:T(1,128)S(1)}, u32[]{:S(2)}, u32[]{:S(2)}) async-start(s32[16,1,4]{2,1,0:T(1,128)} %bitcast.35), calls=%async_computation.1 | async-start | bytes 16384 | tf_op jit(solution)/shard_map/all_to_all | solution.py:83
  121.2 6.4 %collective-permute-start.2 = (f32[256,64]{0,1:T(8,128)S(1)}, f32[256,64]{0,1:T(8,128)S(1)}, u32[]{:S(2)}, u32[]{:S(2)}) collective-permute-start(f32[256,64]{0,1:T(8,128)S(1)} %get-tuple-element.18), channel_id=1, source_target_pairs={{0,1},{1,2},{2,3},{3,4},{4,5},{5,6},{6,7},{7,8},{8,9},{9,10},{10,1... | collective-permute-start | bytes 196616 | tf_op jit(solution)/shard_map/ppermute | solution.py:22
  121.3 6.4 %collective-permute-start.3 = (f32[256,64]{0,1:T(8,128)S(1)}, f32[256,64]{0,1:T(8,128)S(1)}, u32[]{:S(2)}, u32[]{:S(2)}) collective-permute-start(f32[256,64]{0,1:T(8,128)S(1)} %get-tuple-element.19), channel_id=1, source_target_pairs={{1,0},{2,1},{3,2},{4,3},{5,4},{6,5},{7,6},{8,7},{9,8},{10,9},{11,1... | collective-permute-start | bytes 196616 | tf_op jit(solution)/shard_map/ppermute | solution.py:23
  216.9 6.4 %collective-permute-start.4 = (f32[256,64]{0,1:T(8,128)S(1)}, f32[256,64]{0,1:T(8,128)S(1)}, u32[]{:S(2)}, u32[]{:S(2)}) collective-permute-start(f32[256,64]{0,1:T(8,128)S(1)} %get-tuple-element.16), channel_id=1, source_target_pairs={{0,1},{1,2},{2,3},{3,4},{4,5},{5,6},{6,7},{7,8},{8,9},{9,10},{10,1... | collective-permute-start | bytes 196616 | tf_op jit(solution)/shard_map/ppermute | solution.py:22
  217.0 6.4 %collective-permute-start.5 = (f32[256,64]{0,1:T(8,128)S(1)}, f32[256,64]{0,1:T(8,128)S(1)}, u32[]{:S(2)}, u32[]{:S(2)}) collective-permute-start(f32[256,64]{0,1:T(8,128)S(1)} %get-tuple-element.17), channel_id=1, source_target_pairs={{1,0},{2,1},{3,2},{4,3},{5,4},{6,5},{7,6},{8,7},{9,8},{10,9},{11,1... | collective-permute-start | bytes 196616 | tf_op jit(solution)/shard_map/ppermute | solution.py:23
  237.8 89.1 %copy-start.6 = (bf16[128,256]{1,0:T(8,128)(2,1)S(1)}, bf16[128,256]{1,0:T(8,128)(2,1)}, u32[]{:S(2)}) copy-start(bf16[128,256]{1,0:T(8,128)(2,1)} %param.13) | copy-start | bytes 196612
  299.9 36.8 %copy-start.3 = (f32[64,64]{1,0:T(8,128)}, f32[64,64]{1,0:T(8,128)S(1)}, u32[]{:S(2)}) copy-start(f32[64,64]{1,0:T(8,128)S(1)} %psum.23) | copy-start | bytes 49156
  300.5 36.2 %copy-start.2 = (bf16[2048,64]{0,1:T(8,128)(2,1)}, bf16[2048,64]{0,1:T(8,128)(2,1)S(1)}, u32[]{:S(2)}) copy-start(bf16[2048,64]{0,1:T(8,128)(2,1)S(1)} %fusion.10) | copy-start | bytes 786436
  308.1 18.0 %all-to-all-start = ((bf16[16,256,64]{1,2,0:T(8,128)(2,1)}), bf16[16,256,64]{1,2,0:T(8,128)(2,1)S(1)}, u32[]{:S(2)}, u32[]{:S(2)}) async-start(bf16[16,256,64]{1,2,0:T(8,128)(2,1)} %copy.61), calls=%async_computation | async-start | bytes 1048576 | tf_op jit(solution)/shard_map/all_to_all | solution.py:82
  338.1 12.0 %all-to-all-start.2 = ((bf16[16,256,16]{1,2,0:T(8,128)(2,1)}), bf16[16,256,16]{1,2,0:T(8,128)(2,1)S(1)}, u32[]{:S(2)}, u32[]{:S(2)}) async-start(bf16[16,256,16]{1,2,0:T(8,128)(2,1)} %bitcast.162), calls=%async_computation.2 | async-start | bytes 262144 | tf_op jit(solution)/shard_map/all_to_all | solution.py:104
where the time goes:
time: 358 us
  blocking collectives  186 us (52%)
  matrix products  48.1 us (13%)
  other arithmetic  44.1 us (12%)
  local copies, waits for them, and re-layouts  26.5 us (7%)
  waiting for transfers between devices  26.1 us (7%)
  starting transfers between devices  25.7 us (7%)
    psum x2, blocking collectives, gram_factor(): moment = lax.psum(inner_matrix(vectors, vectors), 'rows')  124 us
    psum x1, blocking collectives, on_device(): ritz = lax.psum(inner_matrix(basis, image), 'rows')  62.1 us
    dot_general x3, matrix products, apply_local(): jnp.einsum('btij,btjk->bik', lap_tiles, picked, precision=highest_precision)  33.7 us
    another operation x3, other arithmetic  18.5 us
    all_to_all x1, waiting for transfers between devices, on_device(): lax.all_to_all(outgoing, 'rows', split_axis=0, concat_axis=0, tiled=True)  14.3 us
    ppermute x3, starting transfers between devices, extended(): after = lax.ppermute(initial, axis, down)  13.9 us
    another operation x6, other arithmetic, gram_factor(): return jnp.linalg.cholesky(moment)  13 us
    another operation x4, other arithmetic, apply_inverse(): return jax.scipy.linalg.solve_triangular(factor, vectors.T, lower=True).T  11.1 us
  transfers between devices with their start and end apart: 9, of which 4 were waited for; matrix products, arithmetic and copies ran while one was open for 27% of the time, Pallas kernels for 0%

commit v1 on v0

v1 whole, which is shorter than its diff:
```python
import functools
import math

import jax
import jax.numpy as jnp
from jax import lax
from jax.experimental import pallas as pl
from jax.experimental.pallas import tpu as pltpu
from jax.sharding import PartitionSpec as P

HALO = 2
TILE = 128
K = 64
PATCH_DEV = 4
MESH = pl.DeviceIdType.MESH
F32 = jnp.float32
BF16 = jnp.bfloat16
HIGH = lax.Precision.HIGHEST


def dot(a, b, ca=1, cb=0, precision=None):
    return lax.dot_general(
        a, b, (((ca,), (cb,)), ((), ())), precision=precision, preferred_element_type=F32
    )


def fold(x):
    return x + pltpu.roll(x, K, 1)


def low_lanes(shape):
    return lax.broadcasted_iota(jnp.int32, shape, len(shape) - 1) < K


def halves(x):
    high = x.astype(BF16)
    low = (x - high.astype(F32)).astype(BF16)
    return jnp.where(low_lanes(x.shape), high, low)


def pair_rows(x):
    high = x.astype(BF16)
    low = (x - high.astype(F32)).astype(BF16)
    return jnp.concatenate([high, low], axis=0)


def inner(left, right):
    full = dot(left, right, 0, 0)
    return fold(full[:K] + full[K:])


def inverse_factor(gram):
    lane = lax.broadcasted_iota(jnp.int32, (8, 2 * K), 1)
    sub = lax.broadcasted_iota(jnp.int32, (8, 2 * K), 0)
    slabs = []
    for s in range(K // 8):
        unit = (lane - K == sub + 8 * s).astype(F32)
        slabs.append(jnp.where(lane < K, gram[8 * s:8 * s + 8], unit))
    for k in range(K):
        s, r = divmod(k, 8)
        row = slabs[s][r:r + 1]
        scaled = row * (1.0 / row[:, k:k + 1])
        for j in range(s, K // 8):
            col = slabs[j][:, k:k + 1]
            if j == s:
                if r == 7:
                    continue
                col = jnp.where(sub[:, :1] > r, col, 0.0)
            slabs[j] = slabs[j] - col * scaled
    out = []
    for s in range(K // 8):
        diagonal = jnp.sum(jnp.where(lane == sub + 8 * s, slabs[s], 0.0), axis=1, keepdims=True)
        out.append(slabs[s] * lax.rsqrt(diagonal))
    whole = jnp.concatenate(out, axis=0)
    return jnp.where(low_lanes(whole.shape), pltpu.roll(whole, K, 1), whole)


class Summed:
    def __init__(self, n, me, off, own, recv, total, sems):
        self.n, self.me, self.off = n, me, off
        self.own, self.recv, self.total = own, recv, total
        self.sems = sems
        self.pieces = own.shape[0] // 8
        self.stride = n // self.pieces
        self.mine = lax.div(me, self.stride)
        self.owner = lax.rem(me, self.stride) == off

    def copy(self, src, dst, send, recv, device):
        return pltpu.make_async_remote_copy(
            src_ref=src, dst_ref=dst, send_sem=self.sems.at[send], recv_sem=self.sems.at[recv],
            device_id={"rows": device}, device_id_type=MESH,
        )

    def scatter(self):
        def one(p, carry):
            owner = p * self.stride + self.off
            slot = lax.rem(self.me - owner + self.n, self.n) - 1

            @pl.when(owner != self.me)
            def _():
                self.copy(
                    self.own.at[pl.ds(pl.multiple_of(p * 8, 8), 8)], self.recv.at[slot], 0, 1, owner
                ).start()
            return carry
        lax.fori_loop(0, self.pieces, one, 0, unroll=True)

    def gather(self):
        @pl.when(self.owner)
        def _():
            self.copy(self.recv, self.recv, 0, 1, self.me).wait_recv()
            part = pl.ds(pl.multiple_of(self.mine * 8, 8), 8)
            self.total[part] = self.own[part] + jnp.sum(self.recv[...], axis=0)

            def one(i, carry):
                other = lax.rem(self.me + i, self.n)
                self.copy(self.total.at[part], self.total.at[part], 2, 3, other).start()
                return carry
            lax.fori_loop(1, self.n, one, 0, unroll=self.n <= 16)

    def await_sends(self, count):
        rows = self.own.at[pl.ds(0, 8 * count)]
        self.copy(rows, rows, 0, 1, self.me).wait_send()

    def await_total(self, count):
        if count:
            rows = self.total.at[pl.ds(0, 8 * count)]
            self.copy(rows, rows, 2, 3, self.me).wait_recv()

    def finish(self):
        @pl.when(self.owner)
        def _():
            self.await_total(self.pieces - 1)
            self.await_sends(self.pieces - 1)
            self.copy(self.recv, self.recv, 2, 3, self.me).wait_send()

        @pl.when(jnp.logical_not(self.owner))
        def _():
            self.await_total(self.pieces)
            self.await_sends(self.pieces)


def kernel(
    n, lap, cols, start, ids, mix, cls,
    emb_out, ritz_out, lab_out,
    lap32, pairs, y0, y1, y2, v32, s16, w16,
    g1, g1_recv, g1_sum, g2, g2_recv, g2_sum, r3, r3_recv, r3_sum, pt, pt_recv, pt_sum,
    lap_sem, halo_send, halo_recv, g1_sem, g2_sem, r3_sem, pt_sem,
):
    blocks, slots = cols.shape
    rows = blocks * TILE
    patches = pt.shape[0]
    me = lax.axis_index("rows")
    right, left = lax.rem(me + 1, n), lax.rem(me + n - 1, n)
    def lap_copy(b):
        return pltpu.make_async_copy(lap.at[b], lap32.at[b], lap_sem.at[b])

    for b in range(blocks):
        lap_copy(b).start()

    barrier = pltpu.get_barrier_semaphore()

    def greet(i, carry):
        pl.semaphore_signal(
            barrier, inc=1, device_id={"rows": lax.rem(me + i, n)}, device_id_type=MESH
        )
        return carry
    lax.fori_loop(1, n, greet, 0)

    def halo(buf, turn):
        def one(src, dst, side, device):
            return pltpu.make_async_remote_copy(
                src_ref=buf.at[pl.ds(src, HALO)], dst_ref=buf.at[pl.ds(dst, HALO)],
                send_sem=halo_send.at[turn, side], recv_sem=halo_recv.at[turn, side],
                device_id={"rows": device}, device_id_type=MESH,
            )
        return one(blocks, 0, 0, right), one(HALO, blocks + HALO, 1, left)

    def block_rows(b):
        return pl.ds(pl.multiple_of(b * TILE, TILE), TILE)

    def stage(b, carry):
        x = start[block_rows(b), :]
        x = jnp.concatenate([x, x], axis=1)
        v32[block_rows(b), :] = x
        y0[b + HALO] = halves(x)
        return carry
    lax.fori_loop(0, blocks, stage, 0, unroll=2)
    pl.semaphore_wait(barrier, n - 1)
    for copy in halo(y0, 0):
        copy.start()

    def split(b, carry):
        lap_copy(b).wait()
        for t in range(slots):
            pairs[b, :, t * TILE:(t + 1) * TILE] = pair_rows(lap32[b, t])
        return carry
    lax.fori_loop(0, blocks, split, 0)

    def image(buf, b):
        picked = []
        for t in range(slots):
            picked.append(buf[cols[b, t]])
        product = dot(pairs[b], jnp.concatenate(picked, axis=0))
        return 4.0 * v32[block_rows(b), :] - fold(product[:TILE] + product[TILE:])

    def sweep(body, first, last):
        def one(b, carry):
            body(b)
            return carry
        lax.fori_loop(first, last, one, 0, unroll=2)

    for copy in halo(y0, 0):
        copy.wait()

    def first_step(b):
        y1[b + HALO] = halves(image(y0, b))
    sweep(first_step, 0, HALO)
    sweep(first_step, blocks - HALO, blocks)
    for copy in halo(y1, 1):
        copy.start()
    sweep(first_step, HALO, blocks - HALO)
    here = y1[HALO:HALO + blocks].reshape(rows, TILE)
    g1[...] = inner(here, here)
    sum1 = Summed(n, me, 0, g1, g1_recv, g1_sum, g1_sem)
    sum1.scatter()

    def lift(b):
        x = y1[b + HALO].astype(F32)
        v32[block_rows(b), :] = fold(x)
    sweep(lift, 0, blocks)
    for copy in halo(y1, 1):
        copy.wait()

    def second_step(b):
        s16[block_rows(b), :] = halves(image(y1, b))
    sweep(second_step, 0, blocks // 2)
    sum1.gather()
    sweep(second_step, blocks // 2, blocks)
    sum1.finish()

    w16[...] = pair_rows(inverse_factor(g1_sum[...]))

    def second_image(b):
        x = fold(dot(s16[block_rows(b), :], w16[...], 1, 1))
        v32[block_rows(b), :] = x
        y2[b + HALO] = halves(x)
    sweep(second_image, 0, HALO)
    sweep(second_image, blocks - HALO, blocks)
    for copy in halo(y2, 2):
        copy.start()
    sweep(second_image, HALO, blocks - HALO)
    here = y2[HALO:HALO + blocks].reshape(rows, TILE)
    g2[...] = inner(here, here)
    sum2 = Summed(n, me, 0, g2, g2_recv, g2_sum, g2_sem)
    sum2.scatter()

    def members(b):
        who = lax.broadcasted_iota(jnp.int32, (patches, TILE), 0)
        return (who == ids[pl.ds(b, 1), :]).astype(F32)

    def patch_step(b, carry):
        sums, counts = carry
        member = members(b)
        return (
            sums + dot(member.astype(BF16), y2[b + HALO]),
            counts + member,
        )
    zero = jnp.zeros((patches, TILE), F32)
    sums, counts = lax.fori_loop(0, blocks, patch_step, (zero, zero), unroll=2)
    counts = jnp.sum(counts, axis=1, keepdims=True)
    pt[...] = jnp.where(low_lanes((patches, TILE)), fold(sums), counts)
    sum4 = Summed(n, me, 1, pt, pt_recv, pt_sum, pt_sem)
    sum4.scatter()

    for copy in halo(y2, 2):
        copy.wait()

    def third_step(b):
        s16[block_rows(b), :] = halves(image(y2, b))
    sweep(third_step, 0, blocks // 2)
    sum2.gather()
    sweep(third_step, blocks // 2, blocks)
    r3[...] = inner(y2[HALO:HALO + blocks].reshape(rows, TILE), s16[...])
    sum3 = Summed(n, me, 0, r3, r3_recv, r3_sum, r3_sem)
    sum3.scatter()
    sum4.gather()
    sum2.finish()
    factor = inverse_factor(g2_sum[...])
    sum3.gather()
    sum4.finish()
    sum3.finish()

    narrow = factor[:, :K]
    ritz = dot(narrow, dot(r3_sum[:, :K], narrow, 1, 1, HIGH), 1, 0, HIGH)
    ritz_out[...] = ritz
    scale = math.sqrt(rows * n)
    to_embed = scale * dot(ritz, factor, 0, 0, HIGH)
    w16[...] = pair_rows(to_embed)
    gathered = pt_sum[...]
    patch_mean = dot(gathered[:, :K], to_embed[:, :K], 1, 1, HIGH) / gathered[:, K:K + 1]
    mean_project = pair_rows(dot(patch_mean.astype(BF16), mix[K:, :]))

    def head(b):
        embedding = fold(dot(y2[b + HALO], w16[...], 1, 1)).astype(BF16)[:, :K]
        emb_out[block_rows(b), :] = embedding
        member = members(b).astype(BF16)
        member = jnp.concatenate([member, member], axis=0)
        before = dot(embedding, mix[:K, :]) + dot(member, mean_project, 0, 0)
        hidden = 0.5 * before * (1.0 + lax.erf(before * math.sqrt(0.5)))
        lab_out[block_rows(b), :] = dot(hidden.astype(BF16), cls[...]).astype(BF16)
    sweep(head, 0, blocks)


def on_device(lap_tiles, tile_columns, start_block, patch_of, mix_weight, class_weight):
    n = lax.axis_size("rows")
    blocks, slots = tile_columns.shape
    rows = blocks * TILE
    patches = PATCH_DEV * n
    classes = class_weight.shape[1]
    vmem = pl.BlockSpec(memory_space=pltpu.VMEM)
    near = (tile_columns - (lax.axis_index("rows") * blocks - HALO)) % (blocks * n)

    def summed(height):
        return [
            pltpu.VMEM((height, TILE), F32),
            pltpu.VMEM((n - 1, 8, TILE), F32),
            pltpu.VMEM((height, TILE), F32),
        ]
    dma = pltpu.SemaphoreType.DMA
    padded = pltpu.VMEM((blocks + 2 * HALO, TILE, TILE), BF16)
    return pl.pallas_call(
        functools.partial(kernel, n),
        out_shape=(
            jax.ShapeDtypeStruct((rows, K), BF16),
            jax.ShapeDtypeStruct((K, K), F32),
            jax.ShapeDtypeStruct((rows, classes), BF16),
        ),
        in_specs=[
            pl.BlockSpec(memory_space=pl.ANY),
            pl.BlockSpec(memory_space=pltpu.SMEM),
            vmem, vmem, vmem, vmem,
        ],
        out_specs=(vmem, vmem, vmem),
        scratch_shapes=[
            pltpu.VMEM((blocks, slots, TILE, TILE), F32),
            pltpu.VMEM((blocks, 2 * TILE, slots * TILE), BF16),
            padded, padded, padded,
            pltpu.VMEM((rows, TILE), F32),
            pltpu.VMEM((rows, TILE), BF16),
            pltpu.VMEM((TILE, TILE), BF16),
            *summed(K), *summed(K), *summed(K), *summed(patches),
            dma((blocks,)), dma((3, 2)), dma((3, 2)),
            dma((4,)), dma((4,)), dma((4,)), dma((4,)),
        ],
        compiler_params=pltpu.CompilerParams(
            collective_id=0, has_side_effects=True, vmem_limit_bytes=48 * 1024 * 1024
        ),
    )(
        lap_tiles, near, start_block, patch_of.reshape(blocks, TILE),
        mix_weight, class_weight,
    )


def solution(mesh):
    in_specs = (
        P(("parts", "rows"), None, None, None),
        P(("parts", "rows"), None),
        P(("parts", "rows"), None),
        P(("parts", "rows"), None),
        P(),
        P(),
    )
    out_specs = (P(("parts", "rows"), None), P("parts", None), P(("parts", "rows"), None))
    return jax.shard_map(
        on_device, mesh=mesh, in_specs=in_specs, out_specs=out_specs, check_vma=False
    )
```

time: 358 us -> 64.3 us (0.18)
  blocking collectives: 186 us -> 0 us
  Pallas kernels: 0 us -> 56.5 us
  matrix products: 48.1 us -> 0 us
  other arithmetic: 44.1 us -> 0.01 us
  waiting for transfers between devices: 26.1 us -> 0 us
  starting transfers between devices: 25.7 us -> 0 us
  local copies, waits for them, and re-layouts: 26.5 us -> 6.81 us
    psum x3 -> x0, blocking collectives: 186 us -> none  [the longest x2 124 us: gram_factor(): moment = lax.psum(inner_matrix(vectors, vectors), 'rows')]
    pallas_call x0 -> x1, Pallas kernels: none -> 56.5 us  [on_device(): pl.pallas_call(functools.partial(kernel, n), out_shape=(jax.ShapeDtypeStr...]
    dot_general x11 -> x0, matrix products: 46.8 us -> none  [the longest x3 33.7 us: apply_local(): jnp.einsum('btij,btjk->bik', lap_tiles, picked, precision=highest_precision)]
    another operation x13 -> x0, other arithmetic: 42.7 us -> none
    all_to_all x3 -> x0, waiting for transfers between devices: 22.2 us -> none  [the longest x1 14.3 us: on_device(): lax.all_to_all(outgoing, 'rows', split_axis=0, concat_axis=0, tiled=True)]
    ppermute x6 -> x0, starting transfers between devices: 14.5 us -> none  [the longest x3 13.9 us: extended(): after = lax.ppermute(initial, axis, down)]
    gather x4 -> x0, local copies, waits for them, and re-layouts: 13.9 us -> none  [the longest x3 7.75 us: apply_local(): picked = padded_blocks[(tile_columns - base_block) % total_blocks]]
    all_to_all x3 -> x0, starting transfers between devices: 11.2 us -> none  [the longest x1 4.02 us: on_device(): lax.all_to_all(scores, 'rows', split_axis=0, concat_axis=0, tiled=True)]
  transfers between devices with their start and end apart: 9 -> 0, of which waited for: 4 -> 0; matrix products, arithmetic and copies ran while one was open for 27% -> 0% of each run, Pallas kernels for 0% -> 0%
where the time goes in v1:
time: 64.3 us; the launch traced here: 64 us
  Pallas kernels  56.5 us (88%)
  local copies, waits for them, and re-layouts  6.81 us (11%)
  between operations  0.66 us (1%)
    pallas_call x1, Pallas kernels, on_device(): pl.pallas_call(functools.partial(kernel, n), out_shape=(jax.ShapeDtypeStr...  56.5 us
    unnamed x8, local copies, waits for them, and re-layouts  5.1 us
    pallas_call x2, local copies, waits for them, and re-layouts, on_device(): pl.pallas_call(functools.partial(kernel, n), out_shape=(jax.ShapeDtypeStr...  1.71 us

profile of v1, /device:TPU:0, one launch (start us, length us, event | category | flops | bytes accessed | tf_op | source)
XLA Modules:
  0.0 64.0 jit_solution(3973902101407438125)
XLA Ops:
  0.6 0.8 %copy.9 = s32[16,7]{1,0:T(8,128)S(1)} copy(s32[16,7]{0,1:T(8,128)} %param.7) | data formatting | bytes 896 | tf_op args[1]
  1.4 0.8 %copy.11.cls = bf16[256,16]{1,0:T(8,128)(2,1)S(1)} copy(bf16[256,16]{0,1:T(8,128)(2,1)} %param.11) | data formatting | bytes 16384 | tf_op args[5]
  2.2 1.4 %copy.10.start = f32[2048,64]{1,0:T(8,128)S(1)} copy(f32[2048,64]{0,1:T(8,128)} %param.8) | data formatting | bytes 1048576 | tf_op args[2]
  3.6 0.0 copy-start
  3.6 0.8 %copy-done = bf16[128,256]{1,0:T(8,128)(2,1)S(1)} copy-done((bf16[128,256]{1,0:T(8,128)(2,1)S(1)}, bf16[128,256]{1,0:T(8,128)(2,1)}, u32[]{:S(2)}) %copy-start) | copy-done | bytes 65560
  4.5 0.0 copy-start.1
  4.5 0.7 %copy-done.1 = s32[2048,1]{0,1:T(1,128)S(1)} copy-done((s32[2048,1]{0,1:T(1,128)S(1)}, s32[2048,1]{0,1:T(1,128)}, u32[]{:S(2)}) %copy-start.1) | copy-done | bytes 8216
  5.2 56.5 %shard_map.85 = (bf16[2048,64]{1,0:T(8,128)(2,1)S(1)}, f32[64,64]{1,0:T(8,128)S(1)}, bf16[2048,16]{1,0:T(8,128)(2,1)S(1)}) custom-call(f32[16,7,128,128]{3,2,1,0:T(8,128)} %lap.1, s32[16,7]{1,0:T(8,128)S(1)} %add_select_fusion.cols, f32[2048,64]{1,0:T(8,128)S(1)} %copy.10.start, s32[16,128]{1,0:T(8,128)S(1)} %bitcast.1, bf16[128,256]{1,0:T(8,128)(2,1)S(1)} %copy-done, ...), custom_call_target="tpu_custom_call" | custom-call | tf_op jit(solution)/shard_map/pallas_call | solution.py:331
  61.7 0.9 %copy.12 = bf16[2048,64]{0,1:T(8,128)(2,1)} copy(bf16[2048,64]{1,0:T(8,128)(2,1)S(1)} %get-tuple-element.3) | data formatting | bytes 524288 | tf_op jit(solution)/shard_map/pallas_call | solution.py:331
  62.6 0.8 %copy.13 = bf16[2048,16]{0,1:T(8,128)(2,1)} copy(bf16[2048,16]{1,0:T(8,128)(2,1)S(1)} %get-tuple-element.5) | data formatting | bytes 131072 | tf_op jit(solution)/shard_map/pallas_call | solution.py:331
  63.4 0.6 copy.15
  (1 shorter events, 0.0 us)
Async XLA Ops:
  3.6 0.8 %copy-start = (bf16[128,256]{1,0:T(8,128)(2,1)S(1)}, bf16[128,256]{1,0:T(8,128)(2,1)}, u32[]{:S(2)}) copy-start(bf16[128,256]{1,0:T(8,128)(2,1)} %mix.1) | copy-start | bytes 196612
  4.5 0.7 %copy-start.1 = (s32[2048,1]{0,1:T(1,128)S(1)}, s32[2048,1]{0,1:T(1,128)}, u32[]{:S(2)}) copy-start(s32[2048,1]{0,1:T(1,128)} %param.9) | copy-start | bytes 24580

commit v2 on v1

--- a/solution.py
+++ b/solution.py
@@ -12,6 +12,7 @@
 TILE = 128
 K = 64
 PATCH_DEV = 4
+PANEL = 8
 MESH = pl.DeviceIdType.MESH
 F32 = jnp.float32
 BF16 = jnp.bfloat16
@@ -52,23 +53,29 @@
 def inverse_factor(gram):
     lane = lax.broadcasted_iota(jnp.int32, (8, 2 * K), 1)
     sub = lax.broadcasted_iota(jnp.int32, (8, 2 * K), 0)
+    count = K // 8
     slabs = []
-    for s in range(K // 8):
+    for s in range(count):
         unit = (lane - K == sub + 8 * s).astype(F32)
         slabs.append(jnp.where(lane < K, gram[8 * s:8 * s + 8], unit))
-    for k in range(K):
+    for k in range(0, K, PANEL):
         s, r = divmod(k, 8)
-        row = slabs[s][r:r + 1]
-        scaled = row * (1.0 / row[:, k:k + 1])
-        for j in range(s, K // 8):
-            col = slabs[j][:, k:k + 1]
-            if j == s:
-                if r == 7:
-                    continue
-                col = jnp.where(sub[:, :1] > r, col, 0.0)
-            slabs[j] = slabs[j] - col * scaled
+        spread = [
+            [jnp.broadcast_to(slabs[j][:, k + c:k + c + 1], (8, 2 * K)) for j in range(s, count)]
+            for c in range(PANEL)
+        ]
+        for c in range(PANEL):
+            at = r + c
+            over = 1.0 / spread[c][0][at:at + 1]
+            column = [jnp.where(sub > at, spread[c][0], 0.0)] + spread[c][1:]
+            for e in range(c + 1, PANEL):
+                factor = spread[e][0][at:at + 1] * over
+                spread[e] = [x - y * factor for x, y in zip(spread[e], column)]
+            row = slabs[s][at:at + 1] * over
+            for j in range(s, count):
+                slabs[j] = slabs[j] - column[j - s] * row
     out = []
-    for s in range(K // 8):
+    for s in range(count):
         diagonal = jnp.sum(jnp.where(lane == sub + 8 * s, slabs[s], 0.0), axis=1, keepdims=True)
         out.append(slabs[s] * lax.rsqrt(diagonal))
     whole = jnp.concatenate(out, axis=0)
@@ -140,13 +147,13 @@
 
 
 def kernel(
-    n, lap, cols, start, ids, mix, cls,
+    n, lap, cols, start_in, ids_in, mix_in, cls_in,
     emb_out, ritz_out, lab_out,
-    lap32, pairs, y0, y1, y2, v32, s16, w16,
+    start, ids, mix, cls, lap32, pairs, y0, y1, y2, v32, s16, w16,
     g1, g1_recv, g1_sum, g2, g2_recv, g2_sum, r3, r3_recv, r3_sum, pt, pt_recv, pt_sum,
-    lap_sem, halo_send, halo_recv, g1_sem, g2_sem, r3_sem, pt_sem,
+    in_sem, lap_sem, halo_send, halo_recv, g1_sem, g2_sem, r3_sem, pt_sem,
 ):
-    blocks, slots = cols.shape
+    slots, blocks = cols.shape
     rows = blocks * TILE
     patches = pt.shape[0]
     me = lax.axis_index("rows")
@@ -154,6 +161,13 @@
     def lap_copy(b):
         return pltpu.make_async_copy(lap.at[b], lap32.at[b], lap_sem.at[b])
 
+    inputs = [
+        pltpu.make_async_copy(src, dst, in_sem.at[i])
+        for i, (src, dst) in enumerate(
+            ((start_in, start), (ids_in, ids), (mix_in, mix), (cls_in, cls)))
+    ]
+    for copy in inputs:
+        copy.start()
     for b in range(blocks):
         lap_copy(b).start()
 
@@ -178,9 +192,12 @@
     def block_rows(b):
         return pl.ds(pl.multiple_of(b * TILE, TILE), TILE)
 
+    for copy in inputs:
+        copy.wait()
+
     def stage(b, carry):
-        x = start[block_rows(b), :]
-        x = jnp.concatenate([x, x], axis=1)
+        x = start[:, block_rows(b)]
+        x = jnp.concatenate([x, x], axis=0).T
         v32[block_rows(b), :] = x
         y0[b + HALO] = halves(x)
         return carry
@@ -199,7 +216,7 @@
     def image(buf, b):
         picked = []
         for t in range(slots):
-            picked.append(buf[cols[b, t]])
+            picked.append(buf[cols[t, b]])
         product = dot(pairs[b], jnp.concatenate(picked, axis=0))
         return 4.0 * v32[block_rows(b), :] - fold(product[:TILE] + product[TILE:])
 
@@ -207,7 +224,7 @@
         def one(b, carry):
             body(b)
             return carry
-        lax.fori_loop(first, last, one, 0, unroll=2)
+        lax.fori_loop(first, last, one, 0, unroll=min(4, last - first))
 
     for copy in halo(y0, 0):
         copy.wait()
@@ -254,9 +271,10 @@
     sum2 = Summed(n, me, 0, g2, g2_recv, g2_sum, g2_sem)
     sum2.scatter()
 
-    def members(b):
-        who = lax.broadcasted_iota(jnp.int32, (patches, TILE), 0)
-        return (who == ids[pl.ds(b, 1), :]).astype(F32)
+    def members(b, many=1):
+        who = lax.broadcasted_iota(jnp.int32, (patches, many * TILE), 0)
+        named = jnp.concatenate([ids[pl.ds(b + i, 1), :] for i in range(many)], axis=1)
+        return (who == named).astype(F32)
 
     def patch_step(b, carry):
         sums, counts = carry
@@ -298,17 +316,24 @@
     w16[...] = pair_rows(to_embed)
     gathered = pt_sum[...]
     patch_mean = dot(gathered[:, :K], to_embed[:, :K], 1, 1, HIGH) / gathered[:, K:K + 1]
-    mean_project = pair_rows(dot(patch_mean.astype(BF16), mix[K:, :]))
-
-    def head(b):
-        embedding = fold(dot(y2[b + HALO], w16[...], 1, 1)).astype(BF16)[:, :K]
-        emb_out[block_rows(b), :] = embedding
-        member = members(b).astype(BF16)
+    mean_project = dot(mix[K:, :], patch_mean.astype(BF16), 0, 1)
+    high = mean_project.astype(BF16)
+    low = (mean_project - high.astype(F32)).astype(BF16)
+    weights = jnp.concatenate([high, low], axis=1)
+    chunk = math.gcd(blocks, 4)
+
+    def head(c):
+        at = pl.ds(pl.multiple_of(c * chunk * TILE, TILE), chunk * TILE)
+        vectors = y2[pl.ds(c * chunk + HALO, chunk)].reshape(chunk * TILE, TILE)
+        both = dot(w16[...], vectors, 1, 1)
+        embedding = (both[:K] + both[K:]).astype(BF16)
+        emb_out[:, at] = embedding
+        member = members(c * chunk, chunk).astype(BF16)
         member = jnp.concatenate([member, member], axis=0)
-        before = dot(embedding, mix[:K, :]) + dot(member, mean_project, 0, 0)
+        before = dot(mix[:K, :], embedding, 0, 0) + dot(weights, member)
         hidden = 0.5 * before * (1.0 + lax.erf(before * math.sqrt(0.5)))
-        lab_out[block_rows(b), :] = dot(hidden.astype(BF16), cls[...]).astype(BF16)
-    sweep(head, 0, blocks)
+        lab_out[:, at] = dot(cls[...], hidden.astype(BF16)).astype(BF16)
+    sweep(head, 0, blocks // chunk)
 
 
 def on_device(lap_tiles, tile_columns, start_block, patch_of, mix_weight, class_weight):
@@ -318,7 +343,8 @@
     patches = PATCH_DEV * n
     classes = class_weight.shape[1]
     vmem = pl.BlockSpec(memory_space=pltpu.VMEM)
-    near = (tile_columns - (lax.axis_index("rows") * blocks - HALO)) % (blocks * n)
+    hbm = pl.BlockSpec(memory_space=pltpu.HBM)
+    near = (tile_columns.T - (lax.axis_index("rows") * blocks - HALO)) % (blocks * n)
 
     def summed(height):
         return [
@@ -328,20 +354,22 @@
         ]
     dma = pltpu.SemaphoreType.DMA
     padded = pltpu.VMEM((blocks + 2 * HALO, TILE, TILE), BF16)
-    return pl.pallas_call(
+    embedding, ritz, labels = pl.pallas_call(
         functools.partial(kernel, n),
         out_shape=(
-            jax.ShapeDtypeStruct((rows, K), BF16),
+            jax.ShapeDtypeStruct((K, rows), BF16),
             jax.ShapeDtypeStruct((K, K), F32),
-            jax.ShapeDtypeStruct((rows, classes), BF16),
+            jax.ShapeDtypeStruct((classes, rows), BF16),
         ),
         in_specs=[
-            pl.BlockSpec(memory_space=pl.ANY),
-            pl.BlockSpec(memory_space=pltpu.SMEM),
-            vmem, vmem, vmem, vmem,
+            hbm, pl.BlockSpec(memory_space=pltpu.SMEM), hbm, hbm, hbm, hbm,
         ],
         out_specs=(vmem, vmem, vmem),
         scratch_shapes=[
+            pltpu.VMEM((K, rows), F32),
+            pltpu.VMEM((blocks, TILE), jnp.int32),
+            pltpu.VMEM(mix_weight.shape, BF16),
+            pltpu.VMEM((classes, class_weight.shape[0]), BF16),
             pltpu.VMEM((blocks, slots, TILE, TILE), F32),
             pltpu.VMEM((blocks, 2 * TILE, slots * TILE), BF16),
             padded, padded, padded,
@@ -349,16 +377,17 @@
             pltpu.VMEM((rows, TILE), BF16),
             pltpu.VMEM((TILE, TILE), BF16),
             *summed(K), *summed(K), *summed(K), *summed(patches),
-            dma((blocks,)), dma((3, 2)), dma((3, 2)),
+            dma((4,)), dma((blocks,)), dma((3, 2)), dma((3, 2)),
             dma((4,)), dma((4,)), dma((4,)), dma((4,)),
         ],
         compiler_params=pltpu.CompilerParams(
-            collective_id=0, has_side_effects=True, vmem_limit_bytes=48 * 1024 * 1024
+            collective_id=0, has_side_effects=True, vmem_limit_bytes=63 * 1024 * 1024
         ),
     )(
-        lap_tiles, near, start_block, patch_of.reshape(blocks, TILE),
-        mix_weight, class_weight,
+        lap_tiles, near, start_block.T, patch_of.reshape(blocks, TILE),
+        mix_weight, class_weight.T,
     )
+    return embedding.T, ritz, labels.T
 
 
 def solution(mesh):

time: 64.3 us -> 50.4 us (0.78)
  Pallas kernels: 56.5 us -> 43.7 us
  local copies, waits for them, and re-layouts: 6.81 us -> 4.52 us
  other arithmetic: 0.01 us -> 1.29 us
    pallas_call x1, Pallas kernels: 56.5 us -> 43.7 us  [on_device(): pl.pallas_call(functools.partial(kernel, n), out_shape=(jax.ShapeDtypeStr...]
    pallas_call x2 -> x0, local copies, waits for them, and re-layouts: 1.71 us -> none  [on_device(): pl.pallas_call(functools.partial(kernel, n), out_shape=(jax.ShapeDtypeStr...]
    select_n x1, other arithmetic: 0.01 us -> 1.29 us  [on_device(): (tile_columns.T - (lax.axis_index('rows') * blocks - HALO)) % (blocks * n)]
    unnamed x8 -> x3, local copies, waits for them, and re-layouts: 5.1 us -> 4.52 us
where the time goes in v2:
time: 50.4 us; the launch traced here: 50.1 us
  Pallas kernels  43.7 us (87%)
  local copies, waits for them, and re-layouts  4.52 us (9%)
  other arithmetic  1.29 us (3%)
  between operations  0.64 us (1%)
    pallas_call x1, Pallas kernels, on_device(): pl.pallas_call(functools.partial(kernel, n), out_shape=(jax.ShapeDtypeStr...  43.7 us
    unnamed x3, local copies, waits for them, and re-layouts  4.52 us
    select_n x1, other arithmetic, on_device(): (tile_columns.T - (lax.axis_index('rows') * blocks - HALO)) % (blocks * n)  1.29 us

profile of v2, /device:TPU:0, one launch (start us, length us, event | category | flops | bytes accessed | tf_op | source)
XLA Modules:
  0.0 50.1 jit_solution(1948410072449270393)
XLA Ops:
  0.6 1.3 %add_select_fusion.cols = s32[7,16]{1,0:T(8,128)} fusion(s32[16,7]{0,1:T(8,128)} %param.7, s32[]{:T(128)S(6)} %sub.12), kind=kLoop, calls=%fused_computation | loop fusion | flops 1344 | bytes 900 | tf_op jit(solution)/shard_map/jit(remainder)/select_n | solution.py:347
  1.9 43.7 %shard_map.85 = (bf16[64,2048]{1,0:T(8,128)(2,1)}, f32[64,64]{1,0:T(8,128)}, bf16[16,2048]{1,0:T(8,128)(2,1)}) custom-call(f32[16,7,128,128]{3,2,1,0:T(8,128)} %lap.1, s32[7,16]{1,0:T(8,128)} %add_select_fusion.cols, f32[64,2048]{1,0:T(8,128)} %bitcast.9, s32[16,128]{1,0:T(8,128)} %bitcast.12, bf16[128,256]{1,0:T(8,128)(2,1)} %mix_in.1, bf16[16,256]{1,0:T(8,128)(2,1)} %bitcast.13), custom_call_target="tpu_custom_call" | custom-call | tf_op jit(solution)/shard_map/pallas_call | solution.py:357
  45.6 1.7 %copy.12 = bf16[2048,64]{0,1:T(8,128)(2,1)} copy(bf16[2048,64]{0,1:T(8,128)(2,1)} %bitcast.10) | data formatting | bytes 524288
  47.3 1.4 %copy.13 = f32[64,64]{1,0:T(8,128)} copy(f32[64,64]{1,0:T(8,128)} %get-tuple-element.13) | data formatting | bytes 32768
  48.6 1.5 %copy.14 = bf16[2048,16]{0,1:T(8,128)(2,1)} copy(bf16[2048,16]{0,1:T(8,128)(2,1)} %bitcast.11) | data formatting | bytes 131072

commit v3 on v2

--- a/solution.py
+++ b/solution.py
@@ -147,9 +147,9 @@
 
 
 def kernel(
-    n, lap, cols, start_in, ids_in, mix_in, cls_in,
-    emb_out, ritz_out, lab_out,
-    start, ids, mix, cls, lap32, pairs, y0, y1, y2, v32, s16, w16,
+    n, lap, cols, start_in, ids_in, mix_in,
+    image_out, ritz_out, factor_out, mean_out,
+    start, ids, mix, lap32, pairs, y0, y1, y2, v32, s16, w16,
     g1, g1_recv, g1_sum, g2, g2_recv, g2_sum, r3, r3_recv, r3_sum, pt, pt_recv, pt_sum,
     in_sem, lap_sem, halo_send, halo_recv, g1_sem, g2_sem, r3_sem, pt_sem,
 ):
@@ -164,7 +164,7 @@
     inputs = [
         pltpu.make_async_copy(src, dst, in_sem.at[i])
         for i, (src, dst) in enumerate(
-            ((start_in, start), (ids_in, ids), (mix_in, mix), (cls_in, cls)))
+            ((start_in, start), (ids_in, ids), (mix_in, mix)))
     ]
     for copy in inputs:
         copy.start()
@@ -178,7 +178,7 @@
             barrier, inc=1, device_id={"rows": lax.rem(me + i, n)}, device_id_type=MESH
         )
         return carry
-    lax.fori_loop(1, n, greet, 0)
+    lax.fori_loop(1, n, greet, 0, unroll=n <= 16)
 
     def halo(buf, turn):
         def one(src, dst, side, device):
@@ -213,10 +213,16 @@
         return carry
     lax.fori_loop(0, blocks, split, 0)
 
+    def near(column):
+        whole = blocks * n
+        at = column - me * blocks + HALO
+        at = at & (whole - 1) if whole & (whole - 1) == 0 else lax.rem(at + whole, whole)
+        return jnp.minimum(at, blocks + 2 * HALO - 1)
+
     def image(buf, b):
         picked = []
         for t in range(slots):
-            picked.append(buf[cols[t, b]])
+            picked.append(buf[near(cols[t, b])])
         product = dot(pairs[b], jnp.concatenate(picked, axis=0))
         return 4.0 * v32[block_rows(b), :] - fold(product[:TILE] + product[TILE:])
 
@@ -266,15 +272,16 @@
     for copy in halo(y2, 2):
         copy.start()
     sweep(second_image, HALO, blocks - HALO)
+    kept = pltpu.make_async_copy(y2.at[pl.ds(HALO, blocks)], image_out, in_sem.at[3])
+    kept.start()
     here = y2[HALO:HALO + blocks].reshape(rows, TILE)
     g2[...] = inner(here, here)
     sum2 = Summed(n, me, 0, g2, g2_recv, g2_sum, g2_sem)
     sum2.scatter()
 
-    def members(b, many=1):
-        who = lax.broadcasted_iota(jnp.int32, (patches, many * TILE), 0)
-        named = jnp.concatenate([ids[pl.ds(b + i, 1), :] for i in range(many)], axis=1)
-        return (who == named).astype(F32)
+    def members(b):
+        who = lax.broadcasted_iota(jnp.int32, (patches, TILE), 0)
+        return (who == ids[pl.ds(b, 1), :]).astype(F32)
 
     def patch_step(b, carry):
         sums, counts = carry
@@ -297,11 +304,11 @@
         s16[block_rows(b), :] = halves(image(y2, b))
     sweep(third_step, 0, blocks // 2)
     sum2.gather()
+    sum4.gather()
     sweep(third_step, blocks // 2, blocks)
     r3[...] = inner(y2[HALO:HALO + blocks].reshape(rows, TILE), s16[...])
     sum3 = Summed(n, me, 0, r3, r3_recv, r3_sum, r3_sem)
     sum3.scatter()
-    sum4.gather()
     sum2.finish()
     factor = inverse_factor(g2_sum[...])
     sum3.gather()
@@ -313,27 +320,31 @@
     ritz_out[...] = ritz
     scale = math.sqrt(rows * n)
     to_embed = scale * dot(ritz, factor, 0, 0, HIGH)
-    w16[...] = pair_rows(to_embed)
+    factor_out[...] = pair_rows(to_embed)
     gathered = pt_sum[...]
     patch_mean = dot(gathered[:, :K], to_embed[:, :K], 1, 1, HIGH) / gathered[:, K:K + 1]
     mean_project = dot(mix[K:, :], patch_mean.astype(BF16), 0, 1)
     high = mean_project.astype(BF16)
     low = (mean_project - high.astype(F32)).astype(BF16)
-    weights = jnp.concatenate([high, low], axis=1)
-    chunk = math.gcd(blocks, 4)
-
-    def head(c):
-        at = pl.ds(pl.multiple_of(c * chunk * TILE, TILE), chunk * TILE)
-        vectors = y2[pl.ds(c * chunk + HALO, chunk)].reshape(chunk * TILE, TILE)
-        both = dot(w16[...], vectors, 1, 1)
-        embedding = (both[:K] + both[K:]).astype(BF16)
-        emb_out[:, at] = embedding
-        member = members(c * chunk, chunk).astype(BF16)
-        member = jnp.concatenate([member, member], axis=0)
-        before = dot(mix[:K, :], embedding, 0, 0) + dot(weights, member)
-        hidden = 0.5 * before * (1.0 + lax.erf(before * math.sqrt(0.5)))
-        lab_out[:, at] = dot(cls[...], hidden.astype(BF16)).astype(BF16)
-    sweep(head, 0, blocks // chunk)
+    mean_out[...] = jnp.concatenate([high, low], axis=1)
+    kept.wait()
+
+
+def head(image, ritz, factor, mean, ids, mix, cls, emb_out, ritz_out, lab_out):
+    ritz_out[...] = ritz[...]
+    chunk = image.shape[0]
+    patches = mean.shape[1] // 2
+    both = dot(factor[...], image[...].reshape(chunk * TILE, TILE), 1, 1)
+    embedding = (both[:K] + both[K:]).astype(BF16)
+    emb_out[...] = embedding
+    who = lax.broadcasted_iota(jnp.int32, (patches, chunk * TILE), 0)
+    first = pl.program_id(0) * chunk
+    named = jnp.concatenate([ids[pl.ds(first + i, 1), :] for i in range(chunk)], axis=1)
+    member = (who == named).astype(F32).astype(BF16)
+    member = jnp.concatenate([member, member], axis=0)
+    before = dot(mix[:K, :], embedding, 0, 0) + dot(mean[...], member)
+    hidden = 0.5 * before * (1.0 + lax.erf(before * math.sqrt(0.5)))
+    lab_out[...] = dot(cls[...], hidden.astype(BF16)).astype(BF16)
 
 
 def on_device(lap_tiles, tile_columns, start_block, patch_of, mix_weight, class_weight):
@@ -344,7 +355,7 @@
     classes = class_weight.shape[1]
     vmem = pl.BlockSpec(memory_space=pltpu.VMEM)
     hbm = pl.BlockSpec(memory_space=pltpu.HBM)
-    near = (tile_columns.T - (lax.axis_index("rows") * blocks - HALO)) % (blocks * n)
+    columns = tile_columns.T
 
     def summed(height):
         return [
@@ -354,22 +365,24 @@
         ]
     dma = pltpu.SemaphoreType.DMA
     padded = pltpu.VMEM((blocks + 2 * HALO, TILE, TILE), BF16)
-    embedding, ritz, labels = pl.pallas_call(
+    named = patch_of.reshape(blocks, TILE)
+    hidden = mix_weight.shape[1]
+    image, ritz, factor, mean = pl.pallas_call(
         functools.partial(kernel, n),
         out_shape=(
-            jax.ShapeDtypeStruct((K, rows), BF16),
+            jax.ShapeDtypeStruct((blocks, TILE, TILE), BF16),
             jax.ShapeDtypeStruct((K, K), F32),
-            jax.ShapeDtypeStruct((classes, rows), BF16),
+            jax.ShapeDtypeStruct((TILE, TILE), BF16),
+            jax.ShapeDtypeStruct((hidden, 2 * patches), BF16),
         ),
         in_specs=[
-            hbm, pl.BlockSpec(memory_space=pltpu.SMEM), hbm, hbm, hbm, hbm,
+            hbm, pl.BlockSpec(memory_space=pltpu.SMEM), hbm, hbm, hbm,
         ],
-        out_specs=(vmem, vmem, vmem),
+        out_specs=(hbm, vmem, vmem, vmem),
         scratch_shapes=[
             pltpu.VMEM((K, rows), F32),
             pltpu.VMEM((blocks, TILE), jnp.int32),
             pltpu.VMEM(mix_weight.shape, BF16),
-            pltpu.VMEM((classes, class_weight.shape[0]), BF16),
             pltpu.VMEM((blocks, slots, TILE, TILE), F32),
             pltpu.VMEM((blocks, 2 * TILE, slots * TILE), BF16),
             padded, padded, padded,
@@ -384,9 +397,33 @@
             collective_id=0, has_side_effects=True, vmem_limit_bytes=63 * 1024 * 1024
         ),
     )(
-        lap_tiles, near, start_block.T, patch_of.reshape(blocks, TILE),
-        mix_weight, class_weight.T,
+        lap_tiles, columns, start_block.T, named, mix_weight,
     )
+    chunk = math.gcd(blocks, 4)
+
+    def fixed(shape):
+        return pl.BlockSpec(shape, lambda c: (0, 0))
+
+    embedding, ritz, labels = pl.pallas_call(
+        head,
+        grid=(blocks // chunk,),
+        out_shape=(
+            jax.ShapeDtypeStruct((K, rows), BF16),
+            jax.ShapeDtypeStruct((K, K), F32),
+            jax.ShapeDtypeStruct((classes, rows), BF16),
+        ),
+        in_specs=[
+            pl.BlockSpec((chunk, TILE, TILE), lambda c: (c, 0, 0)),
+            fixed((K, K)), fixed((TILE, TILE)), fixed((hidden, 2 * patches)),
+            fixed((blocks, TILE)), fixed((2 * K, hidden)), fixed((classes, hidden)),
+        ],
+        out_specs=(
+            pl.BlockSpec((K, chunk * TILE), lambda c: (0, c)),
+            fixed((K, K)),
+            pl.BlockSpec((classes, chunk * TILE), lambda c: (0, c)),
+        ),
+        compiler_params=pltpu.CompilerParams(vmem_limit_bytes=63 * 1024 * 1024),
+    )(image, ritz, factor, mean, named, mix_weight, class_weight.T)
     return embedding.T, ritz, labels.T
 
 

time: 50.4 us -> 47.2 us (0.937)
  local copies, waits for them, and re-layouts: 4.52 us -> 0 us
  Pallas kernels: 43.7 us -> 46.3 us
  other arithmetic: 1.29 us -> 0 us
    unnamed x3 -> x0, local copies, waits for them, and re-layouts: 4.52 us -> none
    pallas_call x0 -> x1, Pallas kernels: none -> 4.23 us  [on_device(): pl.pallas_call(head, grid=(blocks // chunk,), out_shape=(jax.ShapeDtypeSt...]
    pallas_call x1, Pallas kernels: 43.7 us -> 42.1 us  [on_device(): pl.pallas_call(functools.partial(kernel, n), out_shape=(jax.ShapeDtypeStr...]
    select_n x1 -> x0, other arithmetic: 1.29 us -> none  [on_device(): (tile_columns.T - (lax.axis_index('rows') * blocks - HALO)) % (blocks * n)]
where the time goes in v3:
time: 47.2 us; the launch traced here: 47 us
  Pallas kernels  46.3 us (98%)
  between operations  0.64 us (1%)
    pallas_call x1, Pallas kernels, on_device(): pl.pallas_call(functools.partial(kernel, n), out_shape=(jax.ShapeDtypeStr...  42.1 us
    pallas_call x1, Pallas kernels, on_device(): pl.pallas_call(head, grid=(blocks // chunk,), out_shape=(jax.ShapeDtypeSt...  4.23 us

profile of v3, /device:TPU:0, one launch (start us, length us, event | category | flops | bytes accessed | tf_op | source)
XLA Modules:
  0.0 47.0 jit_solution(13722679550424068705)
XLA Ops:
  0.6 42.1 %shard_map.85 = (bf16[16,128,128]{2,1,0:T(8,128)(2,1)}, f32[64,64]{1,0:T(8,128)}, bf16[128,128]{1,0:T(8,128)(2,1)}, bf16[256,128]{1,0:T(8,128)(2,1)}) custom-call(f32[16,7,128,128]{3,2,1,0:T(8,128)} %lap.1, s32[7,16]{1,0:T(8,128)} %bitcast.10, f32[64,2048]{1,0:T(8,128)} %bitcast.6, s32[16,128]{1,0:T(8,128)} %bitcast.7, bf16[128,256]{1,0:T(8,128)(2,1)} %mix.1), custom_call_target="tpu_custom_call" | custom-call | tf_op jit(solution)/shard_map/pallas_call | solution.py:370
  42.8 4.2 %shard_map.86 = (bf16[64,2048]{1,0:T(8,128)(2,1)}, f32[64,64]{1,0:T(8,128)}, bf16[16,2048]{1,0:T(8,128)(2,1)}) custom-call(bf16[16,128,128]{2,1,0:T(8,128)(2,1)} %get-tuple-element.10.image, f32[64,64]{1,0:T(8,128)} %get-tuple-element.11.ritz, bf16[128,128]{1,0:T(8,128)(2,1)} %get-tuple-element.12.factor, bf16[256,128]{1,0:T(8,128)(2,1)} %get-tuple-element.13.mean, ...), custom_call_target="tpu_custom_call" | custom-call | tf_op jit(solution)/shard_map/pallas_call | solution.py:407
